TPU v7x, 32 devices: a whole 2x2x4 slice. The times are simulated.
32 devices in a mesh: grp: 2 (over x), date: 16 (over z, y, core).
Axes of the slice: x: 2, y: 2, z: 4, core: 2. Of those that a mesh axis runs over, the one named last changes fastest.
Arguments:
- slc: bfloat16 [16, 2, 128, 2048], P('date', None, 'grp'), parts along dimension 2, may hold values from -6 to 6
- pairs: int32 [64, 2], replicated, may hold values from 0 to 15, as said below
- inverse: bfloat16 [15, 64], replicated, may hold values from -6 to 6
Outputs:
- series: float32 [15, 32, 128], P(None, ('grp', 'date')), parts along dimension 1
There are 2 independent parts, one for each index of `grp`. A program takes and returns all parts, laid end to end along the dimension named above; an argument that names none is the same for every part. Nothing has to cross between parts.
Inputs may be any that keep to these rules, and one draw needn't show every extreme that they name: pairs[p,0] < pairs[p,1] for every pair.
All inputs are finite; a program needn't handle non-finite values.
Results may differ from a plain program's by a relative error of at most 0.0003.
Values may be sent and summed in bfloat16 or wider, within the bound.
A program may use at most 128 MiB of HBM per device.

v0:
```python
import jax
import jax.numpy as jnp
from jax import lax
from jax.sharding import PartitionSpec as P

LOOK_R = 4
LOOK_C = 16


def coherence(first, second):
    first = first.astype(jnp.float32)
    second = second.astype(jnp.float32)
    cross = first[:, 1] * second[:, 0] - first[:, 0] * second[:, 1]
    power_ref = first[:, 0] * first[:, 0] + first[:, 1] * first[:, 1]
    power_sec = second[:, 0] * second[:, 0] + second[:, 1] * second[:, 1]
    stacked = jnp.stack([cross, power_ref, power_sec])
    three, count, rows, cols = stacked.shape
    rowsum = stacked.reshape(three, count, rows // LOOK_R, LOOK_R, cols).sum(axis=3)
    window = (jnp.arange(cols)[:, None] // LOOK_C == jnp.arange(cols // LOOK_C)[None, :]).astype(
        jnp.float32
    )
    looked = jnp.dot(rowsum, window, precision=lax.Precision.HIGHEST)
    return looked[0] / jnp.sqrt(looked[1] * looked[2] + 1e-06)


def invert(inverse, proxy):
    return jnp.einsum(
        "sp,pxy->sxy", inverse.astype(jnp.float32), proxy, precision=lax.Precision.HIGHEST
    )


def per_device(slc, pairs, inverse):
    stripes = lax.all_to_all(slc, "date", split_axis=2, concat_axis=0, tiled=True)
    first = jnp.take(stripes, pairs[:, 0], axis=0)
    second = jnp.take(stripes, pairs[:, 1], axis=0)
    proxy = coherence(first, second)
    return invert(inverse, proxy)


def solution(mesh):
    in_specs = (P("date", None, "grp", None), P(), P())
    out_specs = P(None, ("grp", "date"), None)
    return jax.shard_map(
        per_device, mesh=mesh, in_specs=in_specs, out_specs=out_specs, check_vma=False
    )
```

profile of v0, /device:TPU:0, one launch (start us, length us, event | category | flops | bytes accessed | tf_op | source)
XLA Modules:
  0.0 42.1 jit_solution(5127418015980830979)
XLA Ops:
  0.0 0.0 copy-start
  0.0 0.0 copy-start.1
  0.0 2.4 %copy.26 = bf16[1,2,64,2048]{3,1,0,2:T(2,128)(2,1)} copy(bf16[1,2,64,2048]{3,2,1,0:T(8,128)(2,1)} %param.5) | data formatting | bytes 1048576 | tf_op args[0]
  2.4 7.4 %all-to-all-start = ((bf16[1,2,64,2048]{3,1,0,2:T(2,128)(2,1)}), bf16[1,2,64,2048]{3,1,0,2:T(2,128)(2,1)S(1)}, u32[]{:S(2)}, u32[]{:S(2)}) async-start(bf16[1,2,64,2048]{3,1,0,2:T(2,128)(2,1)} %copy.26), calls=%async_computation | async-start | bytes 1048576 | tf_op jit(solution)/shard_map/all_to_all | solution.py:33
  9.8 0.0 copy-done.1
  9.9 14.4 %all-to-all-done = bf16[1,2,64,2048]{3,1,0,2:T(2,128)(2,1)S(1)} async-done(((bf16[1,2,64,2048]{3,1,0,2:T(2,128)(2,1)}), bf16[1,2,64,2048]{3,1,0,2:T(2,128)(2,1)S(1)}, u32[]{:S(2)}, u32[]{:S(2)}) %all-to-all-start) | async-done | bytes 524320 | tf_op jit(solution)/shard_map/all_to_all | solution.py:33
  24.3 0.3 copy.38
  24.5 2.4 %gather_fusion = bf16[64,2,4,2048]{3,2,1,0:T(4,128)(2,1)S(1)} fusion(bf16[16,2,4,2048]{3,2,1,0:T(4,128)(2,1)S(1)} %bitcast.30, s32[1024]{0:T(1024)S(1)} %pad_clamp_fusion.1), kind=kCustom, calls=%fused_computation.clone | custom fusion | bytes 4194560 | tf_op jit(solution)/shard_map/jit(_take)/gather | solution.py:34
  26.9 3.6 %gather_fusion.1 = bf16[64,2,4,2048]{3,2,1,0:T(4,128)(2,1)} fusion(bf16[16,2,4,2048]{3,2,1,0:T(4,128)(2,1)S(1)} %bitcast.31, s32[1024]{0:T(1024)S(1)} %pad_clamp_fusion), kind=kCustom, calls=%fused_computation.1.clone | custom fusion | bytes 4194560 | tf_op jit(solution)/shard_map/jit(_take)/gather | solution.py:35
  30.5 7.5 %fusion = (f32[64,2,4,2048]{3,0,2,1:T(8,128)S(1)}, f32[64,2,4,2048]{3,0,2,1:T(8,128)S(1)}) fusion(bf16[64,2,4,2048]{3,2,1,0:T(4,128)(2,1)} %gather_fusion.1, pred[64]{0:T(512)(128)(4,1)S(1)} %get-tuple-element.13, bf16[64,2,4,2048]{3,2,1,0:T(4,128)(2,1)S(1)} %gather_fusion, pred[64]{0:T(512)(128)(4,1)S(1)} %get-tuple-element.6), kind=kLoop, calls=%fused_computation.4 | loop fusion | flops 4194304 | bytes 12583040 | tf_op jit(solution)/shard_map/convert_element_type | solution.py:12
  38.0 1.6 %subtract_bitcast_fusion = (f32[1,64,4,2048]{3,1,2,0:T(8,128)S(1)}, f32[1,64,4,2048]{3,1,2,0:T(8,128)S(1)}, f32[1,64,4,2048]{3,1,2,0:T(8,128)S(1)}) fusion(f32[64,2,4,2048]{3,0,2,1:T(8,128)S(1)} %get-tuple-element.15, f32[64,2,4,2048]{3,0,2,1:T(8,128)S(1)} %get-tuple-element.16), kind=kLoop, calls=%fused_computation.9 | loop fusion | flops 4718592 | bytes 14680064 | tf_op jit(solution)/shard_map/sub | solution.py:13
  39.6 0.7 %maximum_reduce_fusion = f32[3,64,2048]{2,1,0:T(8,128)S(1)} fusion(f32[1,64,4,2048]{3,1,2,0:T(8,128)S(1)} %get-tuple-element.12, f32[1,64,4,2048]{3,1,2,0:T(8,128)S(1)} %get-tuple-element.11, f32[1,64,4,2048]{3,1,2,0:T(8,128)S(1)} %get-tuple-element.10), kind=kLoop, calls=%fused_computation.2 | loop fusion | flops 4325376 | bytes 7864320 | tf_op jit(solution)/shard_map/reduce_sum | solution.py:18
  40.3 1.0 %fusion.3 = f32[3,64,128]{2,1,0:T(8,128)S(1)} fusion(f32[3,64,2048]{2,1,0:T(8,128)S(1)} %maximum_reduce_fusion, s32[2048]{0:T(1024)S(1)} %add_select_fusion), kind=kOutput, calls=%fused_computation.13 | convolution fusion | flops 604241920 | bytes 1679360 | tf_op jit(solution)/shard_map/dot_general | solution.py:22
  41.3 0.0 copy-done
  41.3 0.1 convolution_bitcast_fusion
  41.5 0.6 %copy.30 = f32[15,1,128]{2,1,0:T(1,128)} copy(f32[15,1,128]{2,0,1:T(8,128)S(1)} %convolution_bitcast_fusion) | data formatting | bytes 15360 | tf_op jit(solution)/shard_map/sp,pxy->sxy/dot_general | solution.py:27
  (4 shorter events, 0.0 us)
Async XLA Ops:
  0.0 41.3 %copy-start = (bf16[15,64]{1,0:T(8,128)(2,1)S(1)}, bf16[15,64]{1,0:T(8,128)(2,1)}, u32[]{:S(2)}) copy-start(bf16[15,64]{1,0:T(8,128)(2,1)} %param.7) | copy-start | bytes 5764
  0.0 9.8 %copy-start.1 = (s32[64,2]{0,1:T(2,128)S(1)}, s32[64,2]{0,1:T(2,128)}, u32[]{:S(2)}) copy-start(s32[64,2]{0,1:T(2,128)} %param.6) | copy-start | bytes 1540
  2.4 21.9 %all-to-all-start = ((bf16[1,2,64,2048]{3,1,0,2:T(2,128)(2,1)}), bf16[1,2,64,2048]{3,1,0,2:T(2,128)(2,1)S(1)}, u32[]{:S(2)}, u32[]{:S(2)}) async-start(bf16[1,2,64,2048]{3,1,0,2:T(2,128)(2,1)} %copy.26), calls=%async_computation | async-start | bytes 1048576 | tf_op jit(solution)/shard_map/all_to_all | solution.py:33
where the time goes:
time: 42.4 us; the launch traced here: 42.1 us
  waiting for transfers between devices  14.4 us (34%)
  other arithmetic  9.83 us (23%)
  local copies, waits for them, and re-layouts  9.23 us (22%)
  starting transfers between devices  7.39 us (17%)
  matrix products  1.16 us (3%)
    all_to_all x1, waiting for transfers between devices, per_device(): lax.all_to_all(slc, 'date', split_axis=2, concat_axis=0, tiled=True)  14.4 us
    convert_element_type x1, other arithmetic, coherence(): second = second.astype(jnp.float32)  7.53 us
    all_to_all x1, starting transfers between devices, per_device(): lax.all_to_all(slc, 'date', split_axis=2, concat_axis=0, tiled=True)  7.39 us
    gather x1, local copies, waits for them, and re-layouts, per_device(): second = jnp.take(stripes, pairs[:, 1], axis=0)  3.56 us
    unnamed x5, local copies, waits for them, and re-layouts  2.41 us
    gather x1, local copies, waits for them, and re-layouts, per_device(): first = jnp.take(stripes, pairs[:, 0], axis=0)  2.36 us
    sub x1, other arithmetic, coherence(): cross = first[:, 1] * second[:, 0] - first[:, 0] * second[:, 1]  1.62 us
    dot_general x1, matrix products, coherence(): looked = jnp.dot(rowsum, window, precision=lax.Precision.HIGHEST)  1.03 us
  transfers between devices with their start and end apart: 1, of which 1 were waited for; matrix products, arithmetic and copies ran while one was open for 0% of the time, Pallas kernels for 0%

commit v1 on v0

v1 whole, which is shorter than its diff:
```python
import functools

import jax
import jax.numpy as jnp
from jax import lax
from jax.experimental import pallas as pl
from jax.experimental.pallas import tpu as pltpu
from jax.sharding import PartitionSpec as P

LOOK_R = 4
LOOK_C = 16
LANES = 128
BLOCK = 16


def split(x):
    high = x.astype(jnp.bfloat16)
    low = (x - high.astype(jnp.float32)).astype(jnp.bfloat16)
    return high, low


def kernel(
    n,
    slc_hbm,
    pairs_hbm,
    inverse_hbm,
    out_ref,
    tile,
    pairs,
    pairs_v,
    inverse,
    stage,
    send,
    recv,
    wide,
    rowsum,
    window,
    in_sem,
    small_sem,
    own_sem,
    send_sem,
    recv_sem,
):
    me = lax.axis_index("date")
    half = n // 2
    rows, cols = tile.shape[1], tile.shape[2]
    chunks = cols // LANES
    blocks = rows // BLOCK
    near = blocks // 2
    per = BLOCK // LOOK_R
    npair = pairs.shape[1]
    base = (me // half) * half
    other = half - base
    block_base = (me // half) * near
    block_other = near - block_base

    def load(k):
        at = pl.ds(pl.multiple_of(block_at(k) * BLOCK, BLOCK), BLOCK)
        return pltpu.make_async_copy(
            slc_hbm.at[0, :, at, :], tile.at[:, at, :], in_sem.at[k]
        )

    def block_at(k):
        if isinstance(k, int):
            first = block_other if k < near else block_base
        else:
            first = jnp.where(k < near, block_other, block_base)
        return first + (me // per + k) % near

    smalls = [
        pltpu.make_async_copy(pairs_hbm, pairs, small_sem.at[0]),
        pltpu.make_async_copy(pairs_hbm, pairs_v, small_sem.at[1]),
        pltpu.make_async_copy(inverse_hbm, inverse, small_sem.at[2]),
    ]
    for k in range(blocks):
        load(k).start()
    for copy in smalls:
        copy.start()

    barrier = pltpu.get_barrier_semaphore()

    def greet(k, _):
        pl.semaphore_signal(
            barrier, inc=1, device_id={"date": (me + k) % n}, device_id_type=pl.DeviceIdType.MESH
        )
        return 0

    lax.fori_loop(1, n, greet, 0)

    def regroup(k):
        block = block_at(k)
        at = pl.ds(pl.multiple_of(block * BLOCK, BLOCK), BLOCK)
        for part in range(2):
            for c in range(chunks):
                piece = tile[part, at, c * LANES : (c + 1) * LANES].astype(jnp.float32)
                stage[part, pl.ds(c, BLOCK, stride=chunks), :] = piece
        for j in range(per):
            for part in range(2):
                span = LOOK_R * chunks
                send[block * per + j, part] = stage[
                    part, j * span : (j + 1) * span, :
                ].astype(jnp.bfloat16)

    def remote(to, came):
        return pltpu.make_async_remote_copy(
            src_ref=send.at[to],
            dst_ref=recv.at[came],
            send_sem=send_sem.at[to],
            recv_sem=recv_sem.at[came],
            device_id={"date": to},
            device_id_type=pl.DeviceIdType.MESH,
        )

    def post(k):
        block = block_at(k)
        for j in range(per):
            to = block * per + (me + j) % per

            @pl.when(to != me)
            def _():
                remote(to, me).start()

    load(0).wait()
    regroup(0)
    pl.semaphore_wait(barrier, n - 1)
    post(0)

    def rest(k, _):
        load(k).wait()
        regroup(k)
        post(k)
        return 0

    lax.fori_loop(1, blocks, rest, 0)

    for copy in smalls:
        copy.wait()

    col = lax.broadcasted_iota(jnp.int32, (cols, cols // LOOK_C), 0) // LOOK_C
    win = lax.broadcasted_iota(jnp.int32, (cols, cols // LOOK_C), 1)
    window[...] = jnp.where(col == win, 1.0, 0.0).astype(jnp.bfloat16)

    def over_rows(x):
        return x.reshape(LOOK_R, chunks, LANES).sum(axis=0)

    def widen(source, block):
        x = block.astype(jnp.float32)
        wide[source] = x
        rowsum[npair + source] = over_rows(x[0] * x[0] + x[1] * x[1])

    widen(me, send[me])

    def arrive(k, _):
        source = jnp.where(k < half, other + (me + k) % half, base + (me + k + 1) % half)
        remote(source, source).wait_recv()
        widen(source, recv[source])
        return 0

    lax.fori_loop(0, n - 1, arrive, 0)

    def pair(p, _):
        a = pairs[0, p]
        b = pairs[1, p]
        cross = wide[a, 1] * wide[b, 0] - wide[a, 0] * wide[b, 1]
        rowsum[p] = over_rows(cross)
        return 0

    lax.fori_loop(0, npair, pair, 0, unroll=4)

    total = npair + n
    looked = jnp.zeros((total, cols // LOOK_C), jnp.float32)
    for c in range(chunks):
        high, low = split(rowsum[:, c, :])
        weight = window[c * LANES : (c + 1) * LANES, :]
        looked += jnp.dot(high, weight, preferred_element_type=jnp.float32)
        looked += jnp.dot(low, weight, preferred_element_type=jnp.float32)
    powers = looked[npair:]
    date = lax.broadcasted_iota(jnp.int32, (n, npair), 0)

    def pick(which):
        hot = jnp.where(pairs_v[which : which + 1, :] == date, 1.0, 0.0)
        return lax.dot_general(
            hot,
            powers,
            (((0,), (0,)), ((), ())),
            precision=lax.Precision.HIGHEST,
            preferred_element_type=jnp.float32,
        )

    proxy = looked[:npair] / jnp.sqrt(pick(0) * pick(1) + 1e-06)
    high, low = split(proxy)
    series = jnp.dot(inverse[...], high, preferred_element_type=jnp.float32)
    series += jnp.dot(inverse[...], low, preferred_element_type=jnp.float32)
    out_ref[...] = series.reshape(out_ref.shape)

    def left(k, _):
        remote((me + k) % n, me).wait_send()
        return 0

    lax.fori_loop(1, n, left, 0)


def per_device(n, slc, pairs, inverse):
    _, _, rows, cols = slc.shape
    steps, npair = inverse.shape
    chunks = cols // LANES
    span = LOOK_R * chunks
    pairs = pairs.T
    return pl.pallas_call(
        functools.partial(kernel, n),
        out_shape=jax.ShapeDtypeStruct((steps, 1, cols // LOOK_C), jnp.float32),
        in_specs=[pl.BlockSpec(memory_space=pltpu.HBM)] * 3,
        out_specs=pl.BlockSpec(memory_space=pltpu.VMEM),
        scratch_shapes=[
            pltpu.VMEM((2, rows, cols), jnp.bfloat16),
            pltpu.SMEM((2, npair), jnp.int32),
            pltpu.VMEM((2, npair), jnp.int32),
            pltpu.VMEM((steps, npair), jnp.bfloat16),
            pltpu.VMEM((2, BLOCK * chunks, LANES), jnp.float32),
            pltpu.VMEM((n, 2, span, LANES), jnp.bfloat16),
            pltpu.VMEM((n, 2, span, LANES), jnp.bfloat16),
            pltpu.VMEM((n, 2, span, LANES), jnp.float32),
            pltpu.VMEM((npair + n, chunks, LANES), jnp.float32),
            pltpu.VMEM((cols, cols // LOOK_C), jnp.bfloat16),
            pltpu.SemaphoreType.DMA((rows // BLOCK,)),
            pltpu.SemaphoreType.DMA((3,)),
            pltpu.SemaphoreType.DMA,
            pltpu.SemaphoreType.DMA((n,)),
            pltpu.SemaphoreType.DMA((n,)),
        ],
        compiler_params=pltpu.CompilerParams(
            collective_id=0, has_side_effects=True, vmem_limit_bytes=48 * 1024 * 1024
        ),
    )(slc, pairs, inverse)


def solution(mesh):
    n = mesh.shape["date"]
    in_specs = (P("date", None, "grp", None), P(), P())
    out_specs = P(None, ("grp", "date"), None)
    return jax.shard_map(
        functools.partial(per_device, n),
        mesh=mesh,
        in_specs=in_specs,
        out_specs=out_specs,
        check_vma=False,
    )
```

time: 42.4 us -> 23.5 us (0.55)
  the two profiles are of different devices: /device:TPU:0 before, /device:TPU:13 now
where the time goes in v1:
time: 23.5 us; the launch traced here: 23.3 us
  Pallas kernels  20.2 us (86%)
  local copies, waits for them, and re-layouts  3 us (13%)
    pallas_call x1, Pallas kernels, per_device(): pl.pallas_call(functools.partial(kernel, n), out_shape=jax.ShapeDtypeStru...  20.2 us
    unnamed x7, local copies, waits for them, and re-layouts  3 us

profile of v1, /device:TPU:13, one launch (start us, length us, event | category | flops | bytes accessed | tf_op | source)
XLA Modules:
  0.0 23.3 jit_solution(6442431489405846282)
XLA Ops:
  0.0 0.0 copy-start.2
  0.0 0.7 %copy-done.2 = s32[64,2]{0,1:T(2,128)S(1)} copy-done((s32[64,2]{0,1:T(2,128)S(1)}, s32[64,2]{0,1:T(2,128)}, u32[]{:S(2)}) %copy-start.2) | copy-done | bytes 536
  0.7 0.0 copy-start
  0.7 1.0 %copy-done = bf16[1,2,64,2048]{3,2,1,0:T(8,128)(2,1)S(1)} copy-done((bf16[1,2,64,2048]{3,2,1,0:T(8,128)(2,1)S(1)}, bf16[1,2,64,2048]{3,2,1,0:T(8,128)(2,1)}, u32[]{:S(2)}) %copy-start) | copy-done | bytes 524312
  1.7 0.0 copy-start.1
  1.7 0.7 %copy-done.1 = bf16[15,64]{1,0:T(8,128)(2,1)S(1)} copy-done((bf16[15,64]{1,0:T(8,128)(2,1)S(1)}, bf16[15,64]{1,0:T(8,128)(2,1)}, u32[]{:S(2)}) %copy-start.1) | copy-done | bytes 1944
  2.4 20.2 %shard_map.37 = f32[15,1,128]{2,1,0:T(1,128)S(1)} custom-call(bf16[1,2,64,2048]{3,2,1,0:T(8,128)(2,1)S(1)} %copy-done, s32[2,64]{1,0:T(2,128)S(1)} %bitcast.1, bf16[15,64]{1,0:T(8,128)(2,1)S(1)} %copy-done.1), custom_call_target="tpu_custom_call" | custom-call | tf_op jit(solution)/shard_map/pallas_call | solution.py:209
  22.7 0.6 %copy.5 = f32[15,1,128]{2,1,0:T(1,128)} copy(f32[15,1,128]{2,1,0:T(1,128)S(1)} %shard_map.37) | data formatting | bytes 15360
Async XLA Ops:
  0.0 0.7 %copy-start.2 = (s32[64,2]{0,1:T(2,128)S(1)}, s32[64,2]{0,1:T(2,128)}, u32[]{:S(2)}) copy-start(s32[64,2]{0,1:T(2,128)} %param.4) | copy-start | bytes 1540
  0.7 1.0 %copy-start = (bf16[1,2,64,2048]{3,2,1,0:T(8,128)(2,1)S(1)}, bf16[1,2,64,2048]{3,2,1,0:T(8,128)(2,1)}, u32[]{:S(2)}) copy-start(bf16[1,2,64,2048]{3,2,1,0:T(8,128)(2,1)} %slc_hbm.1) | copy-start | bytes 1572868
  1.7 0.7 %copy-start.1 = (bf16[15,64]{1,0:T(8,128)(2,1)S(1)}, bf16[15,64]{1,0:T(8,128)(2,1)}, u32[]{:S(2)}) copy-start(bf16[15,64]{1,0:T(8,128)(2,1)} %inverse_hbm.1) | copy-start | bytes 5764

commit v2 on v1

v2 whole, which is shorter than its diff:
```python
import functools

import jax
import jax.numpy as jnp
from jax import lax
from jax.experimental import pallas as pl
from jax.experimental.pallas import tpu as pltpu
from jax.sharding import PartitionSpec as P

LOOK_R = 4
LOOK_C = 16
LANES = 128
BLOCK = 16
PIECES = 2


def split(x):
    high = x.astype(jnp.bfloat16)
    low = (x - high.astype(jnp.float32)).astype(jnp.bfloat16)
    return high, low


def kernel(
    n,
    pieces,
    slc_hbm,
    pairs_hbm,
    inverse_hbm,
    out_ref,
    tile,
    pairs,
    pairs_v,
    inverse,
    stage,
    send,
    recv,
    wide,
    rowsum,
    window,
    hot,
    in_sem,
    small_sem,
    send_sem,
    recv_sem,
):
    me = lax.axis_index("date")
    half = n // 2
    rows, cols = tile.shape[1], tile.shape[2]
    chunks = cols // LANES // pieces
    span = LOOK_R * chunks
    blocks = rows // BLOCK
    near = blocks // 2
    per = BLOCK // LOOK_R
    npair = pairs.shape[1]
    total = npair + n
    group = rowsum.shape[0] // total
    base = (me // half) * half
    other = half - base
    block_base = (me // half) * near
    block_other = near - block_base

    def block_at(k):
        if isinstance(k, int):
            first = block_other if k < near else block_base
        else:
            first = jnp.where(k < near, block_other, block_base)
        return first + (me // per + k) % near

    def load(k):
        at = pl.ds(pl.multiple_of(block_at(k) * BLOCK, BLOCK), BLOCK)
        return pltpu.make_async_copy(
            slc_hbm.at[0, :, at, :], tile.at[:, at, :], in_sem.at[k]
        )

    smalls = [
        pltpu.make_async_copy(pairs_hbm, pairs, small_sem.at[0]),
        pltpu.make_async_copy(pairs_hbm, pairs_v, small_sem.at[1]),
        pltpu.make_async_copy(inverse_hbm, inverse, small_sem.at[2]),
    ]
    barrier = pltpu.get_barrier_semaphore()

    def greet(k, _):
        pl.semaphore_signal(
            barrier, inc=1, device_id={"date": (me + k) % n}, device_id_type=pl.DeviceIdType.MESH
        )
        return 0

    for k in range(blocks):
        load(k).start()
    lax.fori_loop(1, n, greet, 0)
    for copy in smalls:
        copy.start()

    def regroup(k):
        block = block_at(k)
        at = pl.ds(pl.multiple_of(block * BLOCK, BLOCK), BLOCK)
        for q in range(pieces):
            for part in range(2):
                for c in range(chunks):
                    column = (q * chunks + c) * LANES
                    piece = tile[part, at, column : column + LANES].astype(jnp.float32)
                    stage[q, part, pl.ds(c, BLOCK, stride=chunks), :] = piece
            for j in range(per):
                send[q, block * per + j] = stage[
                    q, :, j * span : (j + 1) * span, :
                ].astype(jnp.bfloat16)

    def remote(q, to, came):
        return pltpu.make_async_remote_copy(
            src_ref=send.at[q, to],
            dst_ref=recv.at[q, came],
            send_sem=send_sem.at[q, to],
            recv_sem=recv_sem.at[q, came],
            device_id={"date": to},
            device_id_type=pl.DeviceIdType.MESH,
        )

    def post(q, k):
        block = block_at(k)
        for j in range(per):
            to = block * per + (me + j) % per

            @pl.when(to != me)
            def _():
                remote(q, to, me).start()

    load(0).wait()
    regroup(0)
    pl.semaphore_wait(barrier, n - 1)
    post(0, 0)

    def rest(k, _):
        load(k).wait()
        regroup(k)
        post(0, k)
        return 0

    lax.fori_loop(1, blocks, rest, 0)

    for q in range(1, pieces):

        def more(k, _):
            post(q, k)
            return 0

        lax.fori_loop(0, blocks, more, 0)

    for copy in smalls:
        copy.wait()

    col = lax.broadcasted_iota(jnp.int32, window.shape, 0) // LOOK_C
    win = lax.broadcasted_iota(jnp.int32, window.shape, 1)
    window[...] = jnp.where(col == win, 1.0, 0.0).astype(jnp.bfloat16)
    date = lax.broadcasted_iota(jnp.int32, (n, npair), 0)
    for which in range(2):
        flag = jnp.where(pairs_v[which : which + 1, :] == date, 1.0, 0.0)
        hot[which * npair : (which + 1) * npair, :] = flag.T.astype(jnp.bfloat16)

    def over_rows(x):
        return x.reshape(-1, group, LANES).sum(axis=0)

    def keep(row, x):
        rowsum[pl.ds(pl.multiple_of(row * group, group), group), :] = over_rows(x)

    looked = jnp.zeros((total, window.shape[1]), jnp.float32)
    for q in range(pieces):

        def widen(source, block):
            x = block.astype(jnp.float32)
            wide[source] = x
            keep(npair + source, x[0] * x[0] + x[1] * x[1])

        def arrive(k, _):
            source = jnp.where(
                k < half, other + (me + k) % half, base + (me + k + 1) % half
            )
            remote(q, source, source).wait_recv()
            widen(source, recv[q, source])
            return 0

        def pair(p, _):
            a = pairs[0, p]
            b = pairs[1, p]
            keep(p, wide[a, 1] * wide[b, 0] - wide[a, 0] * wide[b, 1])
            return 0

        widen(me, send[q, me])
        lax.fori_loop(0, n - 1, arrive, 0)
        lax.fori_loop(0, npair, pair, 0, unroll=8)

        columns = []
        for c in range(chunks):
            x = rowsum[pl.ds(c, total, stride=group), :]
            for again in range(c + chunks, group, chunks):
                x += rowsum[pl.ds(again, total, stride=group), :]
            columns.append(x)
        high, low = split(jnp.concatenate(columns, axis=1))
        depth = chunks * LANES
        sums = jnp.dot(
            jnp.concatenate([high, low], axis=0),
            window[q * depth : (q + 1) * depth, :],
            preferred_element_type=jnp.float32,
        )
        looked += sums[:total] + sums[total:]

    def exact(left, x):
        width = x.shape[1]
        both = jnp.concatenate(split(x), axis=1)
        y = jnp.dot(left, both, preferred_element_type=jnp.float32)
        return y[:, :width] + y[:, width:]

    powers = exact(hot[...], looked[npair:])
    proxy = looked[:npair] / jnp.sqrt(powers[:npair] * powers[npair:] + 1e-06)
    out_ref[...] = exact(inverse[...], proxy).reshape(out_ref.shape)

    def left(k, _):
        for q in range(pieces):
            remote(q, (me + k) % n, me).wait_send()
        return 0

    lax.fori_loop(1, n, left, 0)


def per_device(n, slc, pairs, inverse):
    _, _, rows, cols = slc.shape
    steps, npair = inverse.shape
    pieces = PIECES
    chunks = cols // LANES // pieces
    span = LOOK_R * chunks
    group = max(chunks, 8)
    windows = cols // LOOK_C
    return pl.pallas_call(
        functools.partial(kernel, n, pieces),
        out_shape=jax.ShapeDtypeStruct((steps, 1, windows), jnp.float32),
        in_specs=[pl.BlockSpec(memory_space=pltpu.HBM)] * 3,
        out_specs=pl.BlockSpec(memory_space=pltpu.VMEM),
        scratch_shapes=[
            pltpu.VMEM((2, rows, cols), jnp.bfloat16),
            pltpu.SMEM((2, npair), jnp.int32),
            pltpu.VMEM((2, npair), jnp.int32),
            pltpu.VMEM((steps, npair), jnp.bfloat16),
            pltpu.VMEM((pieces, 2, BLOCK * chunks, LANES), jnp.float32),
            pltpu.VMEM((pieces, n, 2, span, LANES), jnp.bfloat16),
            pltpu.VMEM((pieces, n, 2, span, LANES), jnp.bfloat16),
            pltpu.VMEM((n, 2, span, LANES), jnp.float32),
            pltpu.VMEM(((npair + n) * group, LANES), jnp.float32),
            pltpu.VMEM((cols, windows), jnp.bfloat16),
            pltpu.VMEM((2 * npair, n), jnp.bfloat16),
            pltpu.SemaphoreType.DMA((rows // BLOCK,)),
            pltpu.SemaphoreType.DMA((3,)),
            pltpu.SemaphoreType.DMA((pieces, n)),
            pltpu.SemaphoreType.DMA((pieces, n)),
        ],
        compiler_params=pltpu.CompilerParams(
            collective_id=0, has_side_effects=True, vmem_limit_bytes=63 * 1024 * 1024
        ),
    )(slc, pairs.T, inverse)


def solution(mesh):
    n = mesh.shape["date"]
    in_specs = (P("date", None, "grp", None), P(), P())
    out_specs = P(None, ("grp", "date"), None)
    return jax.shard_map(
        functools.partial(per_device, n),
        mesh=mesh,
        in_specs=in_specs,
        out_specs=out_specs,
        check_vma=False,
    )
```

time: 23.5 us -> 21.3 us (0.906)
  the two profiles are of different devices: /device:TPU:13 before, /device:TPU:0 now
where the time goes in v2:
time: 21.3 us; the launch traced here: 21.1 us
  Pallas kernels  19.8 us (93%)
  local copies, waits for them, and re-layouts  1.29 us (6%)
    pallas_call x1, Pallas kernels, per_device(): pl.pallas_call(functools.partial(kernel, n, pieces), out_shape=jax.ShapeD...  19.8 us
    unnamed x1, local copies, waits for them, and re-layouts  1.29 us

profile of v2, /device:TPU:0, one launch (start us, length us, event | category | flops | bytes accessed | tf_op | source)
XLA Modules:
  0.0 21.1 jit_solution(367220581847950097)
XLA Ops:
  0.0 19.8 %shard_map.37 = f32[15,1,128]{2,1,0:T(1,128)} custom-call(bf16[1,2,64,2048]{3,2,1,0:T(8,128)(2,1)} %slc_hbm.1, s32[2,64]{1,0:T(2,128)} %bitcast.1, bf16[15,64]{1,0:T(8,128)(2,1)} %inverse_hbm.1), custom_call_target="tpu_custom_call" | custom-call | tf_op jit(solution)/shard_map/pallas_call | solution.py:232
  19.8 1.3 %copy.5 = f32[15,1,128]{2,1,0:T(1,128)} copy(f32[15,1,128]{2,1,0:T(1,128)} %shard_map.37) | data formatting | bytes 15360

commit v3 on v2

--- a/solution.py
+++ b/solution.py
@@ -59,12 +59,11 @@
     block_base = (me // half) * near
     block_other = near - block_base
 
+    phase = (me // per) % 2
+
     def block_at(k):
-        if isinstance(k, int):
-            first = block_other if k < near else block_base
-        else:
-            first = jnp.where(k < near, block_other, block_base)
-        return first + (me // per + k) % near
+        first = jnp.where((k + phase) % 2 == 0, block_other, block_base)
+        return first + (me // per + k // 2) % near
 
     def load(k):
         at = pl.ds(pl.multiple_of(block_at(k) * BLOCK, BLOCK), BLOCK)
@@ -231,7 +230,7 @@
     windows = cols // LOOK_C
     return pl.pallas_call(
         functools.partial(kernel, n, pieces),
-        out_shape=jax.ShapeDtypeStruct((steps, 1, windows), jnp.float32),
+        out_shape=pltpu.VMEM((steps, 1, windows), jnp.float32),
         in_specs=[pl.BlockSpec(memory_space=pltpu.HBM)] * 3,
         out_specs=pl.BlockSpec(memory_space=pltpu.VMEM),
         scratch_shapes=[

time: 21.3 us -> 19.9 us (0.934)
  Pallas kernels: 19.8 us -> 19.1 us
  local copies, waits for them, and re-layouts: 1.29 us -> 0.6 us
    unnamed x1, local copies, waits for them, and re-layouts: 1.29 us -> 0.6 us
    pallas_call x1, Pallas kernels: 19.8 us -> 19.1 us  [per_device(): pl.pallas_call(functools.partial(kernel, n, pieces), out_shape=pltpu.VMEM...]
where the time goes in v3:
time: 19.9 us; the launch traced here: 19.7 us
  Pallas kernels  19.1 us (96%)
  local copies, waits for them, and re-layouts  0.6 us (3%)
    pallas_call x1, Pallas kernels, per_device(): pl.pallas_call(functools.partial(kernel, n, pieces), out_shape=pltpu.VMEM...  19.1 us
    unnamed x1, local copies, waits for them, and re-layouts  0.6 us

profile of v3, /device:TPU:0, one launch (start us, length us, event | category | flops | bytes accessed | tf_op | source)
XLA Modules:
  0.0 19.7 jit_solution(9325114638996938189)
XLA Ops:
  0.0 19.1 %shard_map.37 = f32[15,1,128]{2,1,0:T(1,128)S(1)} custom-call(bf16[1,2,64,2048]{3,2,1,0:T(8,128)(2,1)} %slc_hbm.1, s32[2,64]{1,0:T(2,128)} %bitcast.1, bf16[15,64]{1,0:T(8,128)(2,1)} %inverse_hbm.1), custom_call_target="tpu_custom_call" | custom-call | tf_op jit(solution)/shard_map/pallas_call | solution.py:231
  19.1 0.6 %copy.5 = f32[15,1,128]{2,1,0:T(1,128)} copy(f32[15,1,128]{2,1,0:T(1,128)S(1)} %shard_map.37) | data formatting | bytes 15360

commit v4 on v3

--- a/solution.py
+++ b/solution.py
@@ -34,7 +34,7 @@
     stage,
     send,
     recv,
-    wide,
+    held,
     rowsum,
     window,
     hot,
@@ -123,68 +123,70 @@
             def _():
                 remote(q, to, me).start()
 
-    load(0).wait()
-    regroup(0)
-    pl.semaphore_wait(barrier, n - 1)
-    post(0, 0)
-
-    def rest(k, _):
+    def fill(k, _):
         load(k).wait()
         regroup(k)
+
+        @pl.when(k == 0)
+        def _():
+            pl.semaphore_wait(barrier, n - 1)
+
         post(0, k)
         return 0
 
-    lax.fori_loop(1, blocks, rest, 0)
-
-    for q in range(1, pieces):
-
-        def more(k, _):
-            post(q, k)
-            return 0
-
-        lax.fori_loop(0, blocks, more, 0)
+    lax.fori_loop(0, blocks, fill, 0)
+
+    def more(k, _):
+        post(1 + k // blocks, k % blocks)
+        return 0
+
+    lax.fori_loop(0, (pieces - 1) * blocks, more, 0)
 
     for copy in smalls:
         copy.wait()
 
-    col = lax.broadcasted_iota(jnp.int32, window.shape, 0) // LOOK_C
-    win = lax.broadcasted_iota(jnp.int32, window.shape, 1)
-    window[...] = jnp.where(col == win, 1.0, 0.0).astype(jnp.bfloat16)
+    def tile_of_window(c, _):
+        shape = (LANES, window.shape[1])
+        col = c * (LANES // LOOK_C) + lax.broadcasted_iota(jnp.int32, shape, 0) // LOOK_C
+        win = lax.broadcasted_iota(jnp.int32, shape, 1)
+        at = pl.ds(pl.multiple_of(c * LANES, LANES), LANES)
+        window[at, :] = jnp.where(col == win, 1.0, 0.0).astype(jnp.bfloat16)
+        return 0
+
+    lax.fori_loop(0, cols // LANES, tile_of_window, 0)
     date = lax.broadcasted_iota(jnp.int32, (n, npair), 0)
     for which in range(2):
         flag = jnp.where(pairs_v[which : which + 1, :] == date, 1.0, 0.0)
         hot[which * npair : (which + 1) * npair, :] = flag.T.astype(jnp.bfloat16)
-
-    def over_rows(x):
-        return x.reshape(-1, group, LANES).sum(axis=0)
+    for q in range(pieces):
+        recv[q, me] = send[q, me]
 
     def keep(row, x):
-        rowsum[pl.ds(pl.multiple_of(row * group, group), group), :] = over_rows(x)
-
-    looked = jnp.zeros((total, window.shape[1]), jnp.float32)
-    for q in range(pieces):
-
-        def widen(source, block):
-            x = block.astype(jnp.float32)
-            wide[source] = x
-            keep(npair + source, x[0] * x[0] + x[1] * x[1])
-
+        at = pl.ds(pl.multiple_of(row * group, group), group)
+        rowsum[at, :] = x.reshape(-1, group, LANES).sum(axis=0)
+
+    def piece_of(q, looked):
         def arrive(k, _):
             source = jnp.where(
                 k < half, other + (me + k) % half, base + (me + k + 1) % half
             )
             remote(q, source, source).wait_recv()
-            widen(source, recv[q, source])
             return 0
 
+        def power(t, _):
+            held[t] = recv[q, t]
+            x = recv[q, t].astype(jnp.float32)
+            keep(npair + t, x[0] * x[0] + x[1] * x[1])
+            return 0
+
         def pair(p, _):
-            a = pairs[0, p]
-            b = pairs[1, p]
-            keep(p, wide[a, 1] * wide[b, 0] - wide[a, 0] * wide[b, 1])
+            a = held[pairs[0, p]].astype(jnp.float32)
+            b = held[pairs[1, p]].astype(jnp.float32)
+            keep(p, a[1] * b[0] - a[0] * b[1])
             return 0
 
-        widen(me, send[q, me])
         lax.fori_loop(0, n - 1, arrive, 0)
+        lax.fori_loop(0, n, power, 0, unroll=8)
         lax.fori_loop(0, npair, pair, 0, unroll=8)
 
         columns = []
@@ -197,10 +199,13 @@
         depth = chunks * LANES
         sums = jnp.dot(
             jnp.concatenate([high, low], axis=0),
-            window[q * depth : (q + 1) * depth, :],
+            window[pl.ds(pl.multiple_of(q * depth, depth), depth), :],
             preferred_element_type=jnp.float32,
         )
-        looked += sums[:total] + sums[total:]
+        return looked + sums[:total] + sums[total:]
+
+    looked = jnp.zeros((total, window.shape[1]), jnp.float32)
+    looked = lax.fori_loop(0, pieces, piece_of, looked)
 
     def exact(left, x):
         width = x.shape[1]
@@ -209,7 +214,7 @@
         return y[:, :width] + y[:, width:]
 
     powers = exact(hot[...], looked[npair:])
-    proxy = looked[:npair] / jnp.sqrt(powers[:npair] * powers[npair:] + 1e-06)
+    proxy = looked[:npair] * lax.rsqrt(powers[:npair] * powers[npair:] + 1e-06)
     out_ref[...] = exact(inverse[...], proxy).reshape(out_ref.shape)
 
     def left(k, _):
@@ -241,7 +246,7 @@
             pltpu.VMEM((pieces, 2, BLOCK * chunks, LANES), jnp.float32),
             pltpu.VMEM((pieces, n, 2, span, LANES), jnp.bfloat16),
             pltpu.VMEM((pieces, n, 2, span, LANES), jnp.bfloat16),
-            pltpu.VMEM((n, 2, span, LANES), jnp.float32),
+            pltpu.VMEM((n, 2, span, LANES), jnp.bfloat16),
             pltpu.VMEM(((npair + n) * group, LANES), jnp.float32),
             pltpu.VMEM((cols, windows), jnp.bfloat16),
             pltpu.VMEM((2 * npair, n), jnp.bfloat16),

time: 19.9 us -> 19.9 us (level)
  no operation moved by 1% of the time
where the time goes in v4:
time: 19.9 us; the launch traced here: 19.7 us
  Pallas kernels  19.1 us (96%)
  local copies, waits for them, and re-layouts  0.6 us (3%)
    pallas_call x1, Pallas kernels, per_device(): pl.pallas_call(functools.partial(kernel, n, pieces), out_shape=pltpu.VMEM...  19.1 us
    unnamed x1, local copies, waits for them, and re-layouts  0.6 us

profile of v4, /device:TPU:0, one launch (start us, length us, event | category | flops | bytes accessed | tf_op | source)
XLA Modules:
  0.0 19.7 jit_solution(2506891500407721343)
XLA Ops:
  0.0 19.1 %shard_map.37 = f32[15,1,128]{2,1,0:T(1,128)S(1)} custom-call(bf16[1,2,64,2048]{3,2,1,0:T(8,128)(2,1)} %slc_hbm.1, s32[2,64]{1,0:T(2,128)} %bitcast.1, bf16[15,64]{1,0:T(8,128)(2,1)} %inverse_hbm.1), custom_call_target="tpu_custom_call" | custom-call | tf_op jit(solution)/shard_map/pallas_call | solution.py:236
  19.1 0.6 %copy.5 = f32[15,1,128]{2,1,0:T(1,128)} copy(f32[15,1,128]{2,1,0:T(1,128)S(1)} %shard_map.37) | data formatting | bytes 15360

commit v5 on v4

--- a/solution.py
+++ b/solution.py
@@ -56,14 +56,10 @@
     group = rowsum.shape[0] // total
     base = (me // half) * half
     other = half - base
-    block_base = (me // half) * near
-    block_other = near - block_base
-
-    phase = (me // per) % 2
+    block_other = near - (me // half) * near
 
     def block_at(k):
-        first = jnp.where((k + phase) % 2 == 0, block_other, block_base)
-        return first + (me // per + k // 2) % near
+        return (block_other + k) % blocks
 
     def load(k):
         at = pl.ds(pl.multiple_of(block_at(k) * BLOCK, BLOCK), BLOCK)
@@ -114,33 +110,26 @@
             device_id_type=pl.DeviceIdType.MESH,
         )
 
-    def post(q, k):
-        block = block_at(k)
-        for j in range(per):
-            to = block * per + (me + j) % per
-
-            @pl.when(to != me)
-            def _():
-                remote(q, to, me).start()
-
     def fill(k, _):
         load(k).wait()
         regroup(k)
-
-        @pl.when(k == 0)
+        return 0
+
+    lax.fori_loop(0, blocks, fill, 0)
+    pl.semaphore_wait(barrier, n - 1)
+
+    def post(step, _):
+        q = step // half
+        at = (me + step) % half
+        remote(q, other + at, me).start()
+
+        @pl.when(base + at != me)
         def _():
-            pl.semaphore_wait(barrier, n - 1)
-
-        post(0, k)
-        return 0
-
-    lax.fori_loop(0, blocks, fill, 0)
-
-    def more(k, _):
-        post(1 + k // blocks, k % blocks)
-        return 0
-
-    lax.fori_loop(0, (pieces - 1) * blocks, more, 0)
+            remote(q, base + at, me).start()
+
+        return 0
+
+    lax.fori_loop(0, pieces * half, post, 0)
 
     for copy in smalls:
         copy.wait()

time: 19.9 us -> 21.3 us (1.070)
  Pallas kernels: 19.1 us -> 20.5 us
    pallas_call x1, Pallas kernels: 19.1 us -> 20.5 us  [per_device(): pl.pallas_call(functools.partial(kernel, n, pieces), out_shape=pltpu.VMEM...]
where the time goes in v5:
time: 21.3 us; the launch traced here: 21.1 us
  Pallas kernels  20.5 us (96%)
  local copies, waits for them, and re-layouts  0.6 us (3%)
    pallas_call x1, Pallas kernels, per_device(): pl.pallas_call(functools.partial(kernel, n, pieces), out_shape=pltpu.VMEM...  20.5 us
    unnamed x1, local copies, waits for them, and re-layouts  0.6 us

profile of v5, /device:TPU:0, one launch (start us, length us, event | category | flops | bytes accessed | tf_op | source)
XLA Modules:
  0.0 21.1 jit_solution(8861806710459611235)
XLA Ops:
  0.0 20.5 %shard_map.37 = f32[15,1,128]{2,1,0:T(1,128)S(1)} custom-call(bf16[1,2,64,2048]{3,2,1,0:T(8,128)(2,1)} %slc_hbm.1, s32[2,64]{1,0:T(2,128)} %bitcast.1, bf16[15,64]{1,0:T(8,128)(2,1)} %inverse_hbm.1), custom_call_target="tpu_custom_call" | custom-call | tf_op jit(solution)/shard_map/pallas_call | solution.py:225
  20.5 0.6 %copy.5 = f32[15,1,128]{2,1,0:T(1,128)} copy(f32[15,1,128]{2,1,0:T(1,128)S(1)} %shard_map.37) | data formatting | bytes 15360

commit v6 on v4

--- a/solution.py
+++ b/solution.py
@@ -57,13 +57,14 @@
     base = (me // half) * half
     other = half - base
     block_base = (me // half) * near
-    block_other = near - block_base
 
     phase = (me // per) % 2
 
     def block_at(k):
-        first = jnp.where((k + phase) % 2 == 0, block_other, block_base)
-        return first + (me // per + k // 2) % near
+        turn = k // 2
+        far = jnp.where(me < half, blocks - 1 - turn, turn)
+        own = block_base + (me // per + 1 + turn) % near
+        return jnp.where((k + phase) % 2 == 0, far, own)
 
     def load(k):
         at = pl.ds(pl.multiple_of(block_at(k) * BLOCK, BLOCK), BLOCK)
@@ -78,15 +79,15 @@
     ]
     barrier = pltpu.get_barrier_semaphore()
 
-    def greet(k, _):
+    for k in [*range(half, n), *range(1, half)]:
         pl.semaphore_signal(
-            barrier, inc=1, device_id={"date": (me + k) % n}, device_id_type=pl.DeviceIdType.MESH
-        )
-        return 0
-
+            barrier,
+            inc=1,
+            device_id={"date": (me + k) % n},
+            device_id_type=pl.DeviceIdType.MESH,
+        )
     for k in range(blocks):
         load(k).start()
-    lax.fori_loop(1, n, greet, 0)
     for copy in smalls:
         copy.start()
 

time: 19.9 us -> 20.1 us (1.010)
  Pallas kernels: 19.1 us -> 19.4 us
    pallas_call x1, Pallas kernels: 19.1 us -> 19.4 us  [per_device(): pl.pallas_call(functools.partial(kernel, n, pieces), out_shape=pltpu.VMEM...]
where the time goes in v6:
time: 20.1 us; the launch traced here: 20 us
  Pallas kernels  19.4 us (97%)
  local copies, waits for them, and re-layouts  0.6 us (3%)
    pallas_call x1, Pallas kernels, per_device(): pl.pallas_call(functools.partial(kernel, n, pieces), out_shape=pltpu.VMEM...  19.4 us
    unnamed x1, local copies, waits for them, and re-layouts  0.6 us

profile of v6, /device:TPU:0, one launch (start us, length us, event | category | flops | bytes accessed | tf_op | source)
XLA Modules:
  0.0 20.0 jit_solution(3023448429234062406)
XLA Ops:
  0.0 19.4 %shard_map.37 = f32[15,1,128]{2,1,0:T(1,128)S(1)} custom-call(bf16[1,2,64,2048]{3,2,1,0:T(8,128)(2,1)} %slc_hbm.1, s32[2,64]{1,0:T(2,128)} %bitcast.1, bf16[15,64]{1,0:T(8,128)(2,1)} %inverse_hbm.1), custom_call_target="tpu_custom_call" | custom-call | tf_op jit(solution)/shard_map/pallas_call | solution.py:237
  19.4 0.6 %copy.5 = f32[15,1,128]{2,1,0:T(1,128)} copy(f32[15,1,128]{2,1,0:T(1,128)S(1)} %shard_map.37) | data formatting | bytes 15360

commit v7 on v6

--- a/solution.py
+++ b/solution.py
@@ -11,7 +11,7 @@
 LOOK_C = 16
 LANES = 128
 BLOCK = 16
-PIECES = 2
+PIECES = 4
 
 
 def split(x):

time: 20.1 us -> 21.4 us (1.065)
  Pallas kernels: 19.4 us -> 20.6 us
    pallas_call x1, Pallas kernels: 19.4 us -> 20.6 us  [per_device(): pl.pallas_call(functools.partial(kernel, n, pieces), out_shape=pltpu.VMEM...]
where the time goes in v7:
time: 21.4 us; the launch traced here: 21.2 us
  Pallas kernels  20.6 us (96%)
  local copies, waits for them, and re-layouts  0.6 us (3%)
    pallas_call x1, Pallas kernels, per_device(): pl.pallas_call(functools.partial(kernel, n, pieces), out_shape=pltpu.VMEM...  20.6 us
    unnamed x1, local copies, waits for them, and re-layouts  0.6 us

profile of v7, /device:TPU:0, one launch (start us, length us, event | category | flops | bytes accessed | tf_op | source)
XLA Modules:
  0.0 21.2 jit_solution(16929605313007949453)
XLA Ops:
  0.0 20.6 %shard_map.37 = f32[15,1,128]{2,1,0:T(1,128)S(1)} custom-call(bf16[1,2,64,2048]{3,2,1,0:T(8,128)(2,1)} %slc_hbm.1, s32[2,64]{1,0:T(2,128)} %bitcast.1, bf16[15,64]{1,0:T(8,128)(2,1)} %inverse_hbm.1), custom_call_target="tpu_custom_call" | custom-call | tf_op jit(solution)/shard_map/pallas_call | solution.py:237
  20.6 0.6 %copy.5 = f32[15,1,128]{2,1,0:T(1,128)} copy(f32[15,1,128]{2,1,0:T(1,128)S(1)} %shard_map.37) | data formatting | bytes 15360

commit v8 on v6

--- a/solution.py
+++ b/solution.py
@@ -109,9 +109,19 @@
         return pltpu.make_async_remote_copy(
             src_ref=send.at[q, to],
             dst_ref=recv.at[q, came],
-            send_sem=send_sem.at[q, to],
-            recv_sem=recv_sem.at[q, came],
+            send_sem=send_sem.at[q],
+            recv_sem=recv_sem.at[q],
             device_id={"date": to},
+            device_id_type=pl.DeviceIdType.MESH,
+        )
+
+    def every(q):
+        return pltpu.make_async_remote_copy(
+            src_ref=send.at[q, pl.ds(0, n - 1)],
+            dst_ref=recv.at[q, pl.ds(0, n - 1)],
+            send_sem=send_sem.at[q],
+            recv_sem=recv_sem.at[q],
+            device_id={"date": (me + 1) % n},
             device_id_type=pl.DeviceIdType.MESH,
         )
 
@@ -167,13 +177,6 @@
         rowsum[at, :] = x.reshape(-1, group, LANES).sum(axis=0)
 
     def piece_of(q, looked):
-        def arrive(k, _):
-            source = jnp.where(
-                k < half, other + (me + k) % half, base + (me + k + 1) % half
-            )
-            remote(q, source, source).wait_recv()
-            return 0
-
         def power(t, _):
             held[t] = recv[q, t]
             x = recv[q, t].astype(jnp.float32)
@@ -186,7 +189,7 @@
             keep(p, a[1] * b[0] - a[0] * b[1])
             return 0
 
-        lax.fori_loop(0, n - 1, arrive, 0)
+        every(q).wait_recv()
         lax.fori_loop(0, n, power, 0, unroll=8)
         lax.fori_loop(0, npair, pair, 0, unroll=8)
 
@@ -218,12 +221,8 @@
     proxy = looked[:npair] * lax.rsqrt(powers[:npair] * powers[npair:] + 1e-06)
     out_ref[...] = exact(inverse[...], proxy).reshape(out_ref.shape)
 
-    def left(k, _):
-        for q in range(pieces):
-            remote(q, (me + k) % n, me).wait_send()
-        return 0
-
-    lax.fori_loop(1, n, left, 0)
+    for q in range(pieces):
+        every(q).wait_send()
 
 
 def per_device(n, slc, pairs, inverse):
@@ -253,8 +252,8 @@
             pltpu.VMEM((2 * npair, n), jnp.bfloat16),
             pltpu.SemaphoreType.DMA((rows // BLOCK,)),
             pltpu.SemaphoreType.DMA((3,)),
-            pltpu.SemaphoreType.DMA((pieces, n)),
-            pltpu.SemaphoreType.DMA((pieces, n)),
+            pltpu.SemaphoreType.DMA((pieces,)),
+            pltpu.SemaphoreType.DMA((pieces,)),
         ],
         compiler_params=pltpu.CompilerParams(
             collective_id=0, has_side_effects=True, vmem_limit_bytes=63 * 1024 * 1024

time: 20.1 us -> 19.3 us (0.960)
  Pallas kernels: 19.4 us -> 18.6 us
    pallas_call x1, Pallas kernels: 19.4 us -> 18.6 us  [per_device(): pl.pallas_call(functools.partial(kernel, n, pieces), out_shape=pltpu.VMEM...]
where the time goes in v8:
time: 19.3 us; the launch traced here: 19.2 us
  Pallas kernels  18.6 us (96%)
  local copies, waits for them, and re-layouts  0.6 us (3%)
    pallas_call x1, Pallas kernels, per_device(): pl.pallas_call(functools.partial(kernel, n, pieces), out_shape=pltpu.VMEM...  18.6 us
    unnamed x1, local copies, waits for them, and re-layouts  0.6 us

profile of v8, /device:TPU:0, one launch (start us, length us, event | category | flops | bytes accessed | tf_op | source)
XLA Modules:
  0.0 19.2 jit_solution(9472488923395046124)
XLA Ops:
  0.0 18.6 %shard_map.37 = f32[15,1,128]{2,1,0:T(1,128)S(1)} custom-call(bf16[1,2,64,2048]{3,2,1,0:T(8,128)(2,1)} %slc_hbm.1, s32[2,64]{1,0:T(2,128)} %bitcast.1, bf16[15,64]{1,0:T(8,128)(2,1)} %inverse_hbm.1), custom_call_target="tpu_custom_call" | custom-call | tf_op jit(solution)/shard_map/pallas_call | solution.py:236
  18.6 0.6 %copy.5 = f32[15,1,128]{2,1,0:T(1,128)} copy(f32[15,1,128]{2,1,0:T(1,128)S(1)} %shard_map.37) | data formatting | bytes 15360

commit v9 on v8

--- a/solution.py
+++ b/solution.py
@@ -178,14 +178,14 @@
 
     def piece_of(q, looked):
         def power(t, _):
-            held[t] = recv[q, t]
             x = recv[q, t].astype(jnp.float32)
+            held[t] = x
             keep(npair + t, x[0] * x[0] + x[1] * x[1])
             return 0
 
         def pair(p, _):
-            a = held[pairs[0, p]].astype(jnp.float32)
-            b = held[pairs[1, p]].astype(jnp.float32)
+            a = held[pairs[0, p]]
+            b = held[pairs[1, p]]
             keep(p, a[1] * b[0] - a[0] * b[1])
             return 0
 
@@ -246,7 +246,7 @@
             pltpu.VMEM((pieces, 2, BLOCK * chunks, LANES), jnp.float32),
             pltpu.VMEM((pieces, n, 2, span, LANES), jnp.bfloat16),
             pltpu.VMEM((pieces, n, 2, span, LANES), jnp.bfloat16),
-            pltpu.VMEM((n, 2, span, LANES), jnp.bfloat16),
+            pltpu.VMEM((n, 2, span, LANES), jnp.float32),
             pltpu.VMEM(((npair + n) * group, LANES), jnp.float32),
             pltpu.VMEM((cols, windows), jnp.bfloat16),
             pltpu.VMEM((2 * npair, n), jnp.bfloat16),

time: 19.3 us -> 19.3 us (level)
  no operation moved by 1% of the time
where the time goes in v9:
time: 19.3 us; the launch traced here: 19.1 us
  Pallas kernels  18.5 us (96%)
  local copies, waits for them, and re-layouts  0.6 us (3%)
    pallas_call x1, Pallas kernels, per_device(): pl.pallas_call(functools.partial(kernel, n, pieces), out_shape=pltpu.VMEM...  18.5 us
    unnamed x1, local copies, waits for them, and re-layouts  0.6 us

profile of v9, /device:TPU:0, one launch (start us, length us, event | category | flops | bytes accessed | tf_op | source)
XLA Modules:
  0.0 19.1 jit_solution(11871145795280741122)
XLA Ops:
  0.0 18.5 %shard_map.37 = f32[15,1,128]{2,1,0:T(1,128)S(1)} custom-call(bf16[1,2,64,2048]{3,2,1,0:T(8,128)(2,1)} %slc_hbm.1, s32[2,64]{1,0:T(2,128)} %bitcast.1, bf16[15,64]{1,0:T(8,128)(2,1)} %inverse_hbm.1), custom_call_target="tpu_custom_call" | custom-call | tf_op jit(solution)/shard_map/pallas_call | solution.py:236
  18.5 0.6 %copy.5 = f32[15,1,128]{2,1,0:T(1,128)} copy(f32[15,1,128]{2,1,0:T(1,128)S(1)} %shard_map.37) | data formatting | bytes 15360

commit v10 on v9

--- a/solution.py
+++ b/solution.py
@@ -11,7 +11,7 @@
 LOOK_C = 16
 LANES = 128
 BLOCK = 16
-PIECES = 2
+PIECES = 1
 
 
 def split(x):

time: 19.3 us -> 18.4 us (0.953)
  the two profiles are of different devices: /device:TPU:0 before, /device:TPU:9 now
where the time goes in v10:
time: 18.4 us; the launch traced here: 18.3 us
  Pallas kernels  17.7 us (96%)
  local copies, waits for them, and re-layouts  0.6 us (3%)
    pallas_call x1, Pallas kernels, per_device(): pl.pallas_call(functools.partial(kernel, n, pieces), out_shape=pltpu.VMEM...  17.7 us
    unnamed x1, local copies, waits for them, and re-layouts  0.6 us

profile of v10, /device:TPU:9, one launch (start us, length us, event | category | flops | bytes accessed | tf_op | source)
XLA Modules:
  0.0 18.3 jit_solution(9329942041006124798)
XLA Ops:
  0.0 17.7 %shard_map.37 = f32[15,1,128]{2,1,0:T(1,128)S(1)} custom-call(bf16[1,2,64,2048]{3,2,1,0:T(8,128)(2,1)} %slc_hbm.1, s32[2,64]{1,0:T(2,128)} %bitcast.1, bf16[15,64]{1,0:T(8,128)(2,1)} %inverse_hbm.1), custom_call_target="tpu_custom_call" | custom-call | tf_op jit(solution)/shard_map/pallas_call | solution.py:236
  17.7 0.6 %copy.5 = f32[15,1,128]{2,1,0:T(1,128)} copy(f32[15,1,128]{2,1,0:T(1,128)S(1)} %shard_map.37) | data formatting | bytes 15360

commit v11 on v10

--- a/solution.py
+++ b/solution.py
@@ -47,13 +47,14 @@
     half = n // 2
     rows, cols = tile.shape[1], tile.shape[2]
     chunks = cols // LANES // pieces
+    pitch = chunks + 1
     span = LOOK_R * chunks
     blocks = rows // BLOCK
     near = blocks // 2
     per = BLOCK // LOOK_R
     npair = pairs.shape[1]
     total = npair + n
-    group = rowsum.shape[0] // total
+    group = rowsum.shape[0] // total - 1
     base = (me // half) * half
     other = half - base
     block_base = (me // half) * near
@@ -99,28 +100,31 @@
                 for c in range(chunks):
                     column = (q * chunks + c) * LANES
                     piece = tile[part, at, column : column + LANES].astype(jnp.float32)
-                    stage[q, part, pl.ds(c, BLOCK, stride=chunks), :] = piece
-            for j in range(per):
-                send[q, block * per + j] = stage[
-                    q, :, j * span : (j + 1) * span, :
-                ].astype(jnp.bfloat16)
+                    stage[q, part, pl.ds(c, BLOCK, stride=pitch), :] = piece
+            for row in range(BLOCK):
+                for part in range(2):
+                    at = row % LOOK_R * chunks
+                    piece = stage[q, part, row * pitch : row * pitch + chunks, :]
+                    send[q, block * per + row // LOOK_R, part, at : at + chunks] = (
+                        piece.astype(jnp.bfloat16)
+                    )
 
     def remote(q, to, came):
         return pltpu.make_async_remote_copy(
             src_ref=send.at[q, to],
             dst_ref=recv.at[q, came],
             send_sem=send_sem.at[q],
-            recv_sem=recv_sem.at[q],
+            recv_sem=recv_sem.at[q, (to // half + me // half) % 2],
             device_id={"date": to},
             device_id_type=pl.DeviceIdType.MESH,
         )
 
-    def every(q):
+    def every(q, side, count):
         return pltpu.make_async_remote_copy(
-            src_ref=send.at[q, pl.ds(0, n - 1)],
-            dst_ref=recv.at[q, pl.ds(0, n - 1)],
+            src_ref=send.at[q, pl.ds(0, count)],
+            dst_ref=recv.at[q, pl.ds(0, count)],
             send_sem=send_sem.at[q],
-            recv_sem=recv_sem.at[q],
+            recv_sem=recv_sem.at[q, side],
             device_id={"date": (me + 1) % n},
             device_id_type=pl.DeviceIdType.MESH,
         )
@@ -173,15 +177,20 @@
         recv[q, me] = send[q, me]
 
     def keep(row, x):
-        at = pl.ds(pl.multiple_of(row * group, group), group)
-        rowsum[at, :] = x.reshape(-1, group, LANES).sum(axis=0)
+        rowsum[pl.ds(row * (group + 1), group), :] = x.reshape(-1, group, LANES).sum(axis=0)
 
     def piece_of(q, looked):
-        def power(t, _):
+        def power(t):
             x = recv[q, t].astype(jnp.float32)
             held[t] = x
             keep(npair + t, x[0] * x[0] + x[1] * x[1])
-            return 0
+
+        def powers_from(first):
+            def one(k, _):
+                power(first + k)
+                return 0
+
+            lax.fori_loop(0, half, one, 0, unroll=4)
 
         def pair(p, _):
             a = held[pairs[0, p]]
@@ -189,15 +198,17 @@
             keep(p, a[1] * b[0] - a[0] * b[1])
             return 0
 
-        every(q).wait_recv()
-        lax.fori_loop(0, n, power, 0, unroll=8)
+        every(q, 0, half - 1).wait_recv()
+        powers_from(base)
+        every(q, 1, half).wait_recv()
+        powers_from(other)
         lax.fori_loop(0, npair, pair, 0, unroll=8)
 
         columns = []
         for c in range(chunks):
-            x = rowsum[pl.ds(c, total, stride=group), :]
+            x = rowsum[pl.ds(c, total, stride=group + 1), :]
             for again in range(c + chunks, group, chunks):
-                x += rowsum[pl.ds(again, total, stride=group), :]
+                x += rowsum[pl.ds(again, total, stride=group + 1), :]
             columns.append(x)
         high, low = split(jnp.concatenate(columns, axis=1))
         depth = chunks * LANES
@@ -222,7 +233,7 @@
     out_ref[...] = exact(inverse[...], proxy).reshape(out_ref.shape)
 
     for q in range(pieces):
-        every(q).wait_send()
+        every(q, 0, n - 1).wait_send()
 
 
 def per_device(n, slc, pairs, inverse):
@@ -243,17 +254,17 @@
             pltpu.SMEM((2, npair), jnp.int32),
             pltpu.VMEM((2, npair), jnp.int32),
             pltpu.VMEM((steps, npair), jnp.bfloat16),
-            pltpu.VMEM((pieces, 2, BLOCK * chunks, LANES), jnp.float32),
+            pltpu.VMEM((pieces, 2, BLOCK * (chunks + 1), LANES), jnp.float32),
             pltpu.VMEM((pieces, n, 2, span, LANES), jnp.bfloat16),
             pltpu.VMEM((pieces, n, 2, span, LANES), jnp.bfloat16),
             pltpu.VMEM((n, 2, span, LANES), jnp.float32),
-            pltpu.VMEM(((npair + n) * group, LANES), jnp.float32),
+            pltpu.VMEM(((npair + n) * (group + 1), LANES), jnp.float32),
             pltpu.VMEM((cols, windows), jnp.bfloat16),
             pltpu.VMEM((2 * npair, n), jnp.bfloat16),
             pltpu.SemaphoreType.DMA((rows // BLOCK,)),
             pltpu.SemaphoreType.DMA((3,)),
             pltpu.SemaphoreType.DMA((pieces,)),
-            pltpu.SemaphoreType.DMA((pieces,)),
+            pltpu.SemaphoreType.DMA((pieces, 2)),
         ],
         compiler_params=pltpu.CompilerParams(
             collective_id=0, has_side_effects=True, vmem_limit_bytes=63 * 1024 * 1024

time: 18.4 us -> 18.3 us (level)
  the two profiles are of different devices: /device:TPU:9 before, /device:TPU:11 now
where the time goes in v11:
time: 18.3 us; the launch traced here: 18.2 us
  Pallas kernels  17.6 us (96%)
  local copies, waits for them, and re-layouts  0.6 us (3%)
    pallas_call x1, Pallas kernels, per_device(): pl.pallas_call(functools.partial(kernel, n, pieces), out_shape=pltpu.VMEM...  17.6 us
    unnamed x1, local copies, waits for them, and re-layouts  0.6 us

profile of v11, /device:TPU:11, one launch (start us, length us, event | category | flops | bytes accessed | tf_op | source)
XLA Modules:
  0.0 18.2 jit_solution(5885542248819237025)
XLA Ops:
  0.0 17.6 %shard_map.37 = f32[15,1,128]{2,1,0:T(1,128)S(1)} custom-call(bf16[1,2,64,2048]{3,2,1,0:T(8,128)(2,1)} %slc_hbm.1, s32[2,64]{1,0:T(2,128)} %bitcast.1, bf16[15,64]{1,0:T(8,128)(2,1)} %inverse_hbm.1), custom_call_target="tpu_custom_call" | custom-call | tf_op jit(solution)/shard_map/pallas_call | solution.py:247
  17.6 0.6 %copy.5 = f32[15,1,128]{2,1,0:T(1,128)} copy(f32[15,1,128]{2,1,0:T(1,128)S(1)} %shard_map.37) | data formatting | bytes 15360

commit v12 on v11

--- a/solution.py
+++ b/solution.py
@@ -59,13 +59,12 @@
     other = half - base
     block_base = (me // half) * near
 
-    phase = (me // per) % 2
 
     def block_at(k):
         turn = k // 2
         far = jnp.where(me < half, blocks - 1 - turn, turn)
         own = block_base + (me // per + 1 + turn) % near
-        return jnp.where((k + phase) % 2 == 0, far, own)
+        return jnp.where(k % 2 == 0, far, own)
 
     def load(k):
         at = pl.ds(pl.multiple_of(block_at(k) * BLOCK, BLOCK), BLOCK)

time: 18.3 us -> 18.3 us (level)
  the two profiles are of different devices: /device:TPU:11 before, /device:TPU:9 now
where the time goes in v12:
time: 18.3 us; the launch traced here: 18.2 us
  Pallas kernels  17.6 us (96%)
  local copies, waits for them, and re-layouts  0.6 us (3%)
    pallas_call x1, Pallas kernels, per_device(): pl.pallas_call(functools.partial(kernel, n, pieces), out_shape=pltpu.VMEM...  17.6 us
    unnamed x1, local copies, waits for them, and re-layouts  0.6 us

profile of v12, /device:TPU:9, one launch (start us, length us, event | category | flops | bytes accessed | tf_op | source)
XLA Modules:
  0.0 18.2 jit_solution(13336436617995521326)
XLA Ops:
  0.0 17.6 %shard_map.37 = f32[15,1,128]{2,1,0:T(1,128)S(1)} custom-call(bf16[1,2,64,2048]{3,2,1,0:T(8,128)(2,1)} %slc_hbm.1, s32[2,64]{1,0:T(2,128)} %bitcast.1, bf16[15,64]{1,0:T(8,128)(2,1)} %inverse_hbm.1), custom_call_target="tpu_custom_call" | custom-call | tf_op jit(solution)/shard_map/pallas_call | solution.py:246
  17.6 0.6 %copy.5 = f32[15,1,128]{2,1,0:T(1,128)} copy(f32[15,1,128]{2,1,0:T(1,128)S(1)} %shard_map.37) | data formatting | bytes 15360

commit v13 on v12

--- a/solution.py
+++ b/solution.py
@@ -62,7 +62,7 @@
 
     def block_at(k):
         turn = k // 2
-        far = jnp.where(me < half, blocks - 1 - turn, turn)
+        far = jnp.where(me < half, near + turn, turn)
         own = block_base + (me // per + 1 + turn) % near
         return jnp.where(k % 2 == 0, far, own)
 
@@ -201,7 +201,7 @@
         powers_from(base)
         every(q, 1, half).wait_recv()
         powers_from(other)
-        lax.fori_loop(0, npair, pair, 0, unroll=8)
+        lax.fori_loop(0, npair, pair, 0, unroll=16)
 
         columns = []
         for c in range(chunks):

time: 18.3 us -> 18.3 us (level)
  no operation moved by 1% of the time
where the time goes in v13:
time: 18.3 us; the launch traced here: 18.1 us
  Pallas kernels  17.5 us (96%)
  local copies, waits for them, and re-layouts  0.6 us (3%)
    pallas_call x1, Pallas kernels, per_device(): pl.pallas_call(functools.partial(kernel, n, pieces), out_shape=pltpu.VMEM...  17.5 us
    unnamed x1, local copies, waits for them, and re-layouts  0.6 us

profile of v13, /device:TPU:9, one launch (start us, length us, event | category | flops | bytes accessed | tf_op | source)
XLA Modules:
  0.0 18.1 jit_solution(5572325344341979966)
XLA Ops:
  0.0 17.5 %shard_map.37 = f32[15,1,128]{2,1,0:T(1,128)S(1)} custom-call(bf16[1,2,64,2048]{3,2,1,0:T(8,128)(2,1)} %slc_hbm.1, s32[2,64]{1,0:T(2,128)} %bitcast.1, bf16[15,64]{1,0:T(8,128)(2,1)} %inverse_hbm.1), custom_call_target="tpu_custom_call" | custom-call | tf_op jit(solution)/shard_map/pallas_call | solution.py:246
  17.5 0.6 %copy.5 = f32[15,1,128]{2,1,0:T(1,128)} copy(f32[15,1,128]{2,1,0:T(1,128)S(1)} %shard_map.37) | data formatting | bytes 15360
